TPU v7x, 32 devices: a whole 2x2x4 slice. The times are simulated.
32 devices in a mesh: groups: 2 (over y), row: 4 (over z), col: 4 (over x, core).
Axes of the slice: x: 2, y: 2, z: 4, core: 2. Of those that a mesh axis runs over, the one named last changes fastest.
Arguments:
- tokens: bfloat16 [128, 8192], P(('groups', 'row'), 'col'), parts along dimension 0, may hold values from -6 to 6
- gate_weight: bfloat16 [8192, 26624], P('col', 'row'), may hold values from -0.0625 to 0.0625
- up_weight: bfloat16 [8192, 26624], P('col', 'row'), may hold values from -0.0625 to 0.0625
- down_weight: bfloat16 [26624, 8192], P('row', 'col'), may hold values from -0.0390625 to 0.0390625
Outputs:
- mixed: bfloat16 [128, 8192], P(('groups', 'row'), 'col'), parts along dimension 0
There are 2 independent parts, one for each index of `groups`. A program takes and returns all parts, laid end to end along the dimension named above; an argument that names none is the same for every part. Nothing has to cross between parts.
All inputs are finite; a program needn't handle non-finite values.
Results may differ from a plain program's by a relative error of at most 0.019.
Values may be sent and summed in bfloat16 or wider, within the bound.
A program may use at most 192 MiB of HBM per device.

v0:
```python
import jax
import jax.numpy as jnp
from jax import lax
from jax.sharding import PartitionSpec as P


def swiglu(gate, up):
    return (jax.nn.silu(gate) * up).astype(jnp.bfloat16)


def on_device(tokens, gate_weight, up_weight, down_weight):
    local_width = gate_weight.shape[1]
    portion = lax.all_gather(tokens, "row", axis=0, tiled=True)
    gate_part = jnp.dot(portion, gate_weight, preferred_element_type=jnp.float32)
    up_part = jnp.dot(portion, up_weight, preferred_element_type=jnp.float32)
    partials = jnp.concatenate([gate_part, up_part], axis=1)
    summed = lax.psum(partials.astype(jnp.bfloat16), "col").astype(jnp.float32)
    hidden = swiglu(summed[:, :local_width], summed[:, local_width:])
    return lax.psum_scatter(
        jnp.dot(hidden, down_weight, preferred_element_type=jnp.float32).astype(jnp.bfloat16),
        "row",
        scatter_dimension=0,
        tiled=True,
    )


def solution(mesh):
    return jax.shard_map(
        on_device,
        mesh=mesh,
        in_specs=(P(("groups", "row"), "col"), P("col", "row"), P("col", "row"), P("row", "col")),
        out_specs=P(("groups", "row"), "col"),
        check_vma=False,
    )
```

profile of v0, /device:TPU:0, one launch (start us, length us, event | category | flops | bytes accessed | tf_op | source)
XLA Modules:
  0.0 133.4 jit_solution(782859004819414085)
XLA Ops:
  6.5 0.0 all-reduce.2.cloned.1.call-start
  6.5 15.8 %all_gather.3 = bf16[64,2048]{1,0:T(8,128)(2,1)S(1)} all-gather(bf16[16,2048]{1,0:T(8,128)(2,1)} %param.4), channel_id=1, replica_groups=mesh['groups'=2,'row'=4,'col'=4] {'row'}, dimensions={0}, use_global_device_ids=true | all-gather | bytes 327680 | tf_op jit(solution)/shard_map/all_gather | solution.py:13
  22.4 11.3 %convolution_convert_fusion = bf16[64,6656]{1,0:T(8,128)(2,1)S(1)} fusion(bf16[64,2048]{1,0:T(8,128)(2,1)S(1)} %all_gather.3, bf16[2048,6656]{1,0:T(8,128)(2,1)} %param.6), kind=kOutput, calls=%fused_computation | convolution fusion | flops 1745256448 | bytes 28377088 | tf_op jit(solution)/shard_map/dot_general | solution.py:15
  33.7 11.3 %convolution_convert_fusion.1 = bf16[64,6656]{1,0:T(8,128)(2,1)S(1)} fusion(bf16[64,2048]{1,0:T(8,128)(2,1)S(1)} %all_gather.3, bf16[2048,6656]{1,0:T(8,128)(2,1)} %param.5), kind=kOutput, calls=%fused_computation.1 | convolution fusion | flops 1745256448 | bytes 28377088 | tf_op jit(solution)/shard_map/dot_general | solution.py:14
  45.0 1.3 pad_maximum_fusion
  46.3 0.0 all-reduce.2.cloned.1.call-update
  46.3 0.0 reduce-scatter.2.cloned.1.call-start
  46.4 46.6 %all-reduce.2.cloned.1.call-done = bf16[64,13312]{1,0:T(8,128)(2,1)} async-done(((bf16[64,13312]{1,0:T(8,128)(2,1)}), bf16[64,13312]{1,0:T(8,128)(2,1)}) %all-reduce.2.cloned.1.call-update) | async-done | bytes 1703952 | tf_op jit(solution)/shard_map/psum | solution.py:17
  93.0 1.7 %convert_element_type.10 = f32[64,13312]{1,0:T(8,128)S(1)} convert(bf16[64,13312]{1,0:T(8,128)(2,1)} %all-reduce.2.cloned.1.call-done) | non-fusion elementwise | flops 851968 | bytes 5111808 | tf_op jit(solution)/shard_map/convert_element_type | solution.py:17
  94.7 12.0 %convolution_convert_fusion.2 = bf16[64,2048]{1,0:T(8,128)(2,1)} fusion(bf16[6656,2048]{1,0:T(8,128)(2,1)} %param.7, f32[64,13312]{1,0:T(8,128)S(1)} %convert_element_type.10), kind=kOutput, calls=%fused_computation.2 | convolution fusion | flops 1747517440 | bytes 30932992 | tf_op jit(solution)/shard_map/dot_general | solution.py:20
  106.7 0.0 reduce-scatter.2.cloned.1.call-update
  106.7 19.9 %reduce-scatter.2.cloned.1.call-done = bf16[16,2048]{1,0:T(8,128)(2,1)} async-done(((bf16[64,2048]{1,0:T(8,128)(2,1)}), bf16[16,2048]{1,0:T(8,128)(2,1)}) %reduce-scatter.2.cloned.1.call-update) | async-done | bytes 65552 | tf_op jit(solution)/shard_map/reduce_scatter | solution.py:19
Async XLA Ops:
  6.5 86.5 %all-reduce.2.cloned.1.call-start = ((), (), s32[]{:S(2)}) async-start(), calls=%async_computation.1 | async-start | bytes 3407872 | tf_op jit(solution)/shard_map/psum | solution.py:17
  46.3 80.3 %reduce-scatter.2.cloned.1.call-start = ((), (), s32[]{:S(2)}) async-start(), calls=%async_computation.2 | async-start | bytes 327680 | tf_op jit(solution)/shard_map/reduce_scatter | solution.py:19
Sparse Core Ops, SparseCore 0:
  46.5 46.5 all-reduce.1
  106.9 19.6 reduce-scatter.1
where the time goes:
time: 134 us; the launch traced here: 133 us
  waiting for transfers between devices  66.5 us (50%)
  matrix products  34.7 us (26%)
  blocking collectives  15.8 us (12%)
  between operations  13.4 us (10%)
  other arithmetic  2.97 us (2%)
    psum x1, waiting for transfers between devices, on_device(): summed = lax.psum(partials.astype(jnp.bfloat16), 'col').astype(jnp.float32)  46.6 us
    reduce_scatter x1, waiting for transfers between devices, on_device(): lax.psum_scatter(jnp.dot(hidden, down_weight, preferred_element_type=jnp....  19.9 us
    all_gather x1, blocking collectives, on_device(): portion = lax.all_gather(tokens, 'row', axis=0, tiled=True)  15.8 us
    dot_general x1, matrix products, on_device(): jnp.dot(hidden, down_weight, preferred_element_type=jnp.float32)  12 us
    dot_general x1, matrix products, on_device(): jnp.dot(portion, gate_weight, preferred_element_type=jnp.float32)  11.3 us
    dot_general x1, matrix products, on_device(): up_part = jnp.dot(portion, up_weight, preferred_element_type=jnp.float32)  11.3 us
  transfers between devices with their start and end apart: 2, of which 2 were waited for; matrix products, arithmetic and copies ran while one was open for 0% of the time, Pallas kernels for 0%

commit v1 on v0

v1 whole, which is shorter than its diff:
```python
import functools

import jax
import jax.numpy as jnp
from jax import lax
from jax.experimental import pallas as pl
from jax.experimental.pallas import tpu as pltpu
from jax.sharding import PartitionSpec as P

MESH = pl.DeviceIdType.MESH
WIDTH = 256


def swiglu(gate, up):
    return (jax.nn.silu(gate) * up).astype(jnp.bfloat16)


def plain(tokens, gate_weight, up_weight, down_weight):
    local_width = gate_weight.shape[1]
    portion = lax.all_gather(tokens, "row", axis=0, tiled=True)
    gate_part = jnp.dot(portion, gate_weight, preferred_element_type=jnp.float32)
    up_part = jnp.dot(portion, up_weight, preferred_element_type=jnp.float32)
    partials = jnp.concatenate([gate_part, up_part], axis=1)
    summed = lax.psum(partials.astype(jnp.bfloat16), "col").astype(jnp.float32)
    hidden = swiglu(summed[:, :local_width], summed[:, local_width:])
    return lax.psum_scatter(
        jnp.dot(hidden, down_weight, preferred_element_type=jnp.float32).astype(jnp.bfloat16),
        "row",
        scatter_dimension=0,
        tiled=True,
    )


def kernel(
    tok_hbm, gate_hbm, up_hbm, down_hbm, out_ref,
    tok, gate_v, up_v, down_v, pown, cs, cr, sown, xs, xr, hid, acc, obuf, zr, ys, yr,
    own_sem, gate_sem, up_sem, down_sem,
    tz_send, tz_recv, ty_send, ty_recv,
    c_send, c_recv, x_send, x_recv, hx_send, hx_recv, hy_send, hy_recv, hz_send, hz_recv,
    h0_send, h0_recv, h1_send, h1_recv, oz_send, oz_recv, oy_send, oy_recv,
):
    g, r, c = lax.axis_index("groups"), lax.axis_index("row"), lax.axis_index("col")
    x, core = c // 2, c % 2
    core_peer = {"col": x * 2 + (1 - core)}
    x_peer = {"col": (1 - x) * 2 + core}
    y_peer = {"groups": 1 - g}
    others = [(r + k) % 4 for k in (1, 2, 3)]
    b = tok_hbm.shape[0]
    chunks = gate_v.shape[0]
    half = chunks * WIDTH
    out_half = down_v.shape[3]
    T = 8 * b
    q, h = T // 4, T // 2

    def place(group, row):
        return ((group + core) % 2) * 4 + ((row // 2 + x) % 2) * 2 + row % 2

    def slot(group, row):
        return tok.at[place(group, row)]

    barrier = pltpu.get_barrier_semaphore()
    for peer in [core_peer, x_peer, y_peer] + [{"row": o} for o in others]:
        pl.semaphore_signal(barrier, inc=1, device_id=peer, device_id_type=MESH)

    own = pltpu.make_async_copy(tok_hbm, slot(g, r), own_sem)
    own.start()

    def gate_copy(i):
        at = pl.ds(pl.multiple_of(g * half + i * WIDTH, WIDTH), WIDTH)
        return pltpu.make_async_copy(gate_hbm.at[:, at], gate_v.at[i], gate_sem.at[i])

    def up_copy(i):
        at = pl.ds(pl.multiple_of(g * half + i * WIDTH, WIDTH), WIDTH)
        return pltpu.make_async_copy(up_hbm.at[:, at], up_v.at[i], up_sem.at[i])

    def down_copy(side, i):
        source = (g + side) % 2
        rows = pl.ds(pl.multiple_of(source * half + i * WIDTH, WIDTH), WIDTH)
        columns = pl.ds(pl.multiple_of(g * out_half, 128), out_half)
        return pltpu.make_async_copy(down_hbm.at[rows, columns], down_v.at[side, i], down_sem.at[side, i])

    gate_copy(0).start()
    up_copy(0).start()
    pl.semaphore_wait(barrier, 6)

    def send(src, dst, send_sem, recv_sem, peer):
        return pltpu.make_async_remote_copy(
            src_ref=src, dst_ref=dst, send_sem=send_sem, recv_sem=recv_sem,
            device_id=peer, device_id_type=MESH,
        )

    def tok_z(k):
        return send(tok_hbm, slot(g, r), tz_send.at[k - 1], tz_recv.at[k - 1], {"row": (r + k) % 4})

    def tok_z_in(k):
        block = slot(g, (r + 4 - k) % 4)
        return send(block, block, tz_send.at[k - 1], tz_recv.at[k - 1], {"row": (r + k) % 4})

    def tok_y(k):
        block = slot(g, (r + 4 - k) % 4)
        return send(tok_hbm if k == 0 else block, block, ty_send.at[k], ty_recv.at[k], y_peer)

    def tok_y_in(k):
        block = slot(1 - g, (r + 4 - k) % 4)
        return send(block, block, ty_send.at[k], ty_recv.at[k], y_peer)

    for k in (2, 1, 3):
        tok_z(k).start()
    tok_y(0).start()

    def start_weights(i, carry):
        gate_copy(i).start()
        up_copy(i).start()
        return carry

    def start_down(i, carry):
        down_copy(0, i).start()
        down_copy(1, i).start()
        return carry

    lax.fori_loop(1, chunks, start_weights, 0)
    lax.fori_loop(0, chunks, start_down, 0)

    for k in (1, 3, 2):
        tok_z_in(k).wait_recv()
        tok_y(k).start()
    own.wait()
    for k in (0, 1, 3, 2):
        tok_y_in(k).wait_recv()

    acc[...] = jnp.zeros_like(acc)

    def c_copy(i):
        return send(cs.at[i], cr.at[i], c_send.at[i], c_recv.at[i], core_peer)

    def x_copy(i):
        return send(xs.at[i], xr.at[i], x_send.at[i], x_recv.at[i], x_peer)

    def hx_copy(i):
        return send(hid.at[0, i, pl.ds(0, q)], hid.at[0, i, pl.ds(q, q)], hx_send.at[i], hx_recv.at[i], x_peer)

    def hy_copy(i):
        return send(hid.at[0, i, pl.ds(0, q)], hid.at[1, i, pl.ds(0, q)], hy_send.at[i], hy_recv.at[i], y_peer)

    def hz_copy(i):
        return send(hid.at[0, i, pl.ds(q, q)], hid.at[1, i, pl.ds(q, q)], hz_send.at[i], hz_recv.at[i], y_peer)

    def h0_copy(i):
        return send(hid.at[0, i, pl.ds(0, h)], hid.at[0, i, pl.ds(h, h)], h0_send.at[i], h0_recv.at[i], core_peer)

    def h1_copy(i):
        return send(hid.at[1, i, pl.ds(0, h)], hid.at[1, i, pl.ds(h, h)], h1_send.at[i], h1_recv.at[i], core_peer)

    def project(i):
        gate_copy(i).wait()
        up_copy(i).wait()
        t = tok[...].reshape(T, tok.shape[2])
        for side, w in enumerate((gate_v, up_v)):
            p = jnp.dot(t, w[i], preferred_element_type=jnp.float32)
            at = slice(side * WIDTH, (side + 1) * WIDTH)
            pown[i, :, at] = p[:h]
            cs[i, :, at] = p[h:].astype(jnp.bfloat16)
        c_copy(i).start()

    def add_core(i):
        c_copy(i).wait_recv()
        s = pown[i] + cr[i].astype(jnp.float32)
        sown[i] = s[:q]
        xs[i] = s[q:].astype(jnp.bfloat16)
        x_copy(i).start()

    def add_x(i):
        x_copy(i).wait_recv()
        s = sown[i] + xr[i].astype(jnp.float32)
        gate, up = s[:, :WIDTH], s[:, WIDTH:]
        hid[0, i, pl.ds(0, q), :] = (gate / (1.0 + jnp.exp(-gate)) * up).astype(jnp.bfloat16)
        hx_copy(i).start()
        hy_copy(i).start()

    def spread(i):
        hx_copy(i).wait_recv()
        hz_copy(i).start()
        h0_copy(i).start()

    def spread_y(i):
        hy_copy(i).wait_recv()
        hz_copy(i).wait_recv()
        h1_copy(i).start()

    def contract(i):
        down_copy(0, i).wait()
        down_copy(1, i).wait()
        h0_copy(i).wait_recv()
        h1_copy(i).wait_recv()
        acc[...] += jnp.dot(hid[0, i], down_v[0, i], preferred_element_type=jnp.float32) + jnp.dot(
            hid[1, i], down_v[1, i], preferred_element_type=jnp.float32
        )

    stages = ((spread_y, 5), (spread, 4), (add_x, 2), (add_core, 1), (project, 0), (contract, 6))
    depth = 6

    def step(t, carry):
        for stage, lag in stages:
            i = t - lag
            pl.when(jnp.logical_and(i >= 0, i < chunks))(functools.partial(stage, i))
        return carry

    lax.fori_loop(0, chunks + depth, step, 0)

    def oz_copy(k):
        row = (r + k) % 4
        at = ((row // 2 + x) % 2) * 2 + row % 2
        return send(obuf.at[:, at], zr.at[k - 1], oz_send.at[k - 1], oz_recv.at[k - 1], {"row": row})

    obuf[...] = acc[...].astype(jnp.bfloat16).reshape(obuf.shape)
    for k in (2, 1, 3):
        oz_copy(k).start()

    def drain(i, carry):
        for copy in (c_copy, x_copy, hx_copy, hy_copy, hz_copy, h0_copy, h1_copy):
            copy(i).wait_send()
        return carry

    lax.fori_loop(0, chunks, drain, 0)
    for k in (1, 2, 3):
        tok_z(k).wait_send()
    for k in (0, 1, 2, 3):
        tok_y(k).wait_send()

    mine = (r // 2 + x) % 2 * 2 + r % 2
    theirs_at, ours_at = (1 - g + core) % 2, (g + core) % 2

    def rows_of(at):
        first = pl.multiple_of((at * 4 + mine) * b, b)
        return acc[pl.ds(first, b), :]

    for k in (1, 3, 2):
        oz_copy(k).wait_recv()

    def total(at):
        s = rows_of(at)
        for k in range(3):
            s = s + zr[k, at].astype(jnp.float32)
        return s.astype(jnp.bfloat16)

    oy = send(ys, yr, oy_send, oy_recv, y_peer)
    ys[...] = total(theirs_at)
    oy.start()
    out_ref[:, pl.ds(pl.multiple_of(g * out_half, 128), out_half)] = total(ours_at)
    for k in (1, 2, 3):
        oz_copy(k).wait_send()
    oy.wait()
    out_ref[:, pl.ds(pl.multiple_of((1 - g) * out_half, 128), out_half)] = yr[...]


def fused(tokens, gate_weight, up_weight, down_weight):
    b, k = tokens.shape
    units = gate_weight.shape[1]
    n = down_weight.shape[1]
    chunks = units // 2 // WIDTH
    T = 8 * b
    q, h = T // 4, T // 2
    bf16, f32 = jnp.bfloat16, jnp.float32
    dma = pltpu.SemaphoreType.DMA
    per_chunk = dma((chunks,))
    return pl.pallas_call(
        kernel,
        out_shape=jax.ShapeDtypeStruct((b, n), bf16),
        in_specs=[pl.BlockSpec(memory_space=pl.ANY)] * 4,
        out_specs=pl.BlockSpec(memory_space=pltpu.VMEM),
        scratch_shapes=[
            pltpu.VMEM((8, b, k), bf16),
            pltpu.VMEM((chunks, k, WIDTH), bf16),
            pltpu.VMEM((chunks, k, WIDTH), bf16),
            pltpu.VMEM((2, chunks, WIDTH, n // 2), bf16),
            pltpu.VMEM((chunks, h, 2 * WIDTH), f32),
            pltpu.VMEM((chunks, h, 2 * WIDTH), bf16),
            pltpu.VMEM((chunks, h, 2 * WIDTH), bf16),
            pltpu.VMEM((chunks, q, 2 * WIDTH), f32),
            pltpu.VMEM((chunks, q, 2 * WIDTH), bf16),
            pltpu.VMEM((chunks, q, 2 * WIDTH), bf16),
            pltpu.VMEM((2, chunks, T, WIDTH), bf16),
            pltpu.VMEM((T, n // 2), f32),
            pltpu.VMEM((2, 4, b, n // 2), bf16),
            pltpu.VMEM((3, 2, b, n // 2), bf16),
            pltpu.VMEM((b, n // 2), bf16),
            pltpu.VMEM((b, n // 2), bf16),
            dma,
            per_chunk,
            per_chunk,
            dma((2, chunks)),
            dma((3,)),
            dma((3,)),
            dma((4,)),
            dma((4,)),
        ]
        + [per_chunk] * 14
        + [dma((3,)), dma((3,)), dma, dma],
        compiler_params=pltpu.CompilerParams(
            collective_id=0, has_side_effects=True, vmem_limit_bytes=60 * 2**20
        ),
        cost_estimate=pl.CostEstimate(
            flops=3 * T * k * units, bytes_accessed=3 * k * units, transcendentals=q * units // 2
        ),
    )(tokens, gate_weight, up_weight, down_weight)


def fits(mesh, tokens, gate_weight, down_weight):
    s = mesh.shape
    if (s["groups"], s["row"], s["col"]) != (2, 4, 4):
        return False
    b, k = tokens.shape[0] // 8, tokens.shape[1] // 4
    units, n = gate_weight.shape[1] // 4, down_weight.shape[1] // 4
    small = 3 * k * units + 26 * b * units + 24 * b * (k + n)
    return b % 16 == 0 and k % 128 == 0 and units % (2 * WIDTH) == 0 and n % 256 == 0 and small < 56 * 2**20


def solution(mesh):
    specs = dict(
        mesh=mesh,
        in_specs=(P(("groups", "row"), "col"), P("col", "row"), P("col", "row"), P("row", "col")),
        out_specs=P(("groups", "row"), "col"),
        check_vma=False,
    )

    def layer(tokens, gate_weight, up_weight, down_weight):
        body = fused if fits(mesh, tokens, gate_weight, down_weight) else plain
        return jax.shard_map(body, **specs)(tokens, gate_weight, up_weight, down_weight)

    return layer
```

time: 134 us -> 79.8 us (0.60)
  Pallas kernels: 0 us -> 78.2 us
  waiting for transfers between devices: 66.5 us -> 0 us
  matrix products: 34.7 us -> 0 us
  blocking collectives: 15.8 us -> 0 us
  between operations: 13.4 us -> 0.01 us
  other arithmetic: 2.97 us -> 0 us
  local copies, waits for them, and re-layouts: 0 us -> 1.47 us
    pallas_call x0 -> x1, Pallas kernels: none -> 78.2 us  [fused(): pl.pallas_call(kernel, out_shape=jax.ShapeDtypeStruct((b, n), bf16), in_s...]
    psum x1 -> x0, waiting for transfers between devices: 46.6 us -> none  [on_device(): summed = lax.psum(partials.astype(jnp.bfloat16), 'col').astype(jnp.float32)]
    dot_general x3 -> x0, matrix products: 34.7 us -> none  [the longest x1 12 us: on_device(): jnp.dot(hidden, down_weight, preferred_element_type=jnp.float32)]
    reduce_scatter x1 -> x0, waiting for transfers between devices: 19.9 us -> none  [on_device(): lax.psum_scatter(jnp.dot(hidden, down_weight, preferred_element_type=jnp....]
    all_gather x1 -> x0, blocking collectives: 15.8 us -> none  [on_device(): portion = lax.all_gather(tokens, 'row', axis=0, tiled=True)]
    convert_element_type x1 -> x0, other arithmetic: 1.67 us -> none  [on_device(): summed = lax.psum(partials.astype(jnp.bfloat16), 'col').astype(jnp.float32)]
    unnamed x0 -> x1, local copies, waits for them, and re-layouts: none -> 1.47 us
  transfers between devices with their start and end apart: 2 -> 0, of which waited for: 2 -> 0; matrix products, arithmetic and copies ran while one was open for 0% -> 0% of each run, Pallas kernels for 0% -> 0%
where the time goes in v1:
time: 79.8 us; the launch traced here: 79.6 us
  Pallas kernels  78.2 us (98%)
  local copies, waits for them, and re-layouts  1.47 us (2%)
    pallas_call x1, Pallas kernels, fused(): pl.pallas_call(kernel, out_shape=jax.ShapeDtypeStruct((b, n), bf16), in_s...  78.2 us

profile of v1, /device:TPU:0, one launch (start us, length us, event | category | flops | bytes accessed | tf_op | source)
XLA Modules:
  0.0 79.6 jit_solution(12610656065553048763)
XLA Ops:
  0.0 78.2 %shard_map.46 = bf16[16,2048]{1,0:T(8,128)(2,1)} custom-call(bf16[16,2048]{1,0:T(8,128)(2,1)} %tok_hbm.1, bf16[2048,6656]{1,0:T(8,128)(2,1)} %gate_hbm.1, bf16[2048,6656]{1,0:T(8,128)(2,1)} %up_hbm.1, bf16[6656,2048]{1,0:T(8,128)(2,1)} %down_hbm.1), custom_call_target="tpu_custom_call" | custom-call | flops 5234491392 | bytes 40894464 | tf_op jit(solution)/shard_map/pallas_call | solution.py:266
  78.2 1.5 %copy.6 = bf16[16,2048]{1,0:T(8,128)(2,1)} copy(bf16[16,2048]{1,0:T(8,128)(2,1)} %shard_map.46) | data formatting | bytes 131072

commit v2 on v0

--- a/solution.py
+++ b/solution.py
@@ -1,14 +1,22 @@
+import functools
+
 import jax
 import jax.numpy as jnp
 from jax import lax
+from jax.experimental import pallas as pl
+from jax.experimental.pallas import tpu as pltpu
 from jax.sharding import PartitionSpec as P
+
+MESH = pl.DeviceIdType.MESH
+WIDTH = 256
+SLOTS = 11
 
 
 def swiglu(gate, up):
     return (jax.nn.silu(gate) * up).astype(jnp.bfloat16)
 
 
-def on_device(tokens, gate_weight, up_weight, down_weight):
+def plain(tokens, gate_weight, up_weight, down_weight):
     local_width = gate_weight.shape[1]
     portion = lax.all_gather(tokens, "row", axis=0, tiled=True)
     gate_part = jnp.dot(portion, gate_weight, preferred_element_type=jnp.float32)
@@ -24,11 +32,236 @@
     )
 
 
+def kernel(
+    tok_hbm, gate_hbm, up_hbm, down_hbm, out_ref,
+    tok, gate_v, up_v, down_v, pown, cs, cr, sown, xs, xr, hid, acc, obuf, zr,
+    own_sem, gate_sem, up_sem, down_sem, tz_send, tz_recv,
+    c_send, c_recv, x_send, x_recv, hx_send, hx_recv, h0_send, h0_recv, oz_send, oz_recv,
+):
+    g, r, c = lax.axis_index("groups"), lax.axis_index("row"), lax.axis_index("col")
+    x, core = c // 2, c % 2
+    core_peer = {"col": x * 2 + (1 - core)}
+    x_peer = {"col": (1 - x) * 2 + core}
+    b = tok_hbm.shape[0]
+    slots = gate_v.shape[0]
+    chunks = down_v.shape[0]
+    T = 4 * b
+    q, h = b, 2 * b
+
+    def place(row):
+        return ((row // 2 + core) % 2) * 2 + (row % 2 + x) % 2
+
+    barrier = pltpu.get_barrier_semaphore()
+    for peer in [core_peer, x_peer] + [{"row": (r + k) % 4} for k in (1, 2, 3)]:
+        pl.semaphore_signal(barrier, inc=1, device_id=peer, device_id_type=MESH)
+
+    own = pltpu.make_async_copy(tok_hbm, tok.at[place(r)], own_sem)
+    own.start()
+
+    def gate_copy(i):
+        at = pl.ds(pl.multiple_of(i * WIDTH, WIDTH), WIDTH)
+        return pltpu.make_async_copy(gate_hbm.at[:, at], gate_v.at[i % slots], gate_sem.at[i % slots])
+
+    def up_copy(i):
+        at = pl.ds(pl.multiple_of(i * WIDTH, WIDTH), WIDTH)
+        return pltpu.make_async_copy(up_hbm.at[:, at], up_v.at[i % slots], up_sem.at[i % slots])
+
+    def down_copy(i):
+        rows = pl.ds(pl.multiple_of(i * WIDTH, WIDTH), WIDTH)
+        return pltpu.make_async_copy(down_hbm.at[rows], down_v.at[i], down_sem.at[i])
+
+    def start_weights(i, carry):
+        gate_copy(i).start()
+        up_copy(i).start()
+        return carry
+
+    def start_down(i, carry):
+        down_copy(i).start()
+        return carry
+
+    start_weights(0, 0)
+    pl.semaphore_wait(barrier, 5)
+
+    def send(src, dst, send_sem, recv_sem, peer):
+        return pltpu.make_async_remote_copy(
+            src_ref=src, dst_ref=dst, send_sem=send_sem, recv_sem=recv_sem,
+            device_id=peer, device_id_type=MESH,
+        )
+
+    def tok_copy(k):
+        to = {"row": (r + k) % 4}
+        return send(tok_hbm, tok.at[place(r)], tz_send.at[k - 1], tz_recv.at[k - 1], to)
+
+    def tok_in(k):
+        block = tok.at[place((r + 4 - k) % 4)]
+        return send(block, block, tz_send.at[k - 1], tz_recv.at[k - 1], {"row": (r + k) % 4})
+
+    for k in (2, 1, 3):
+        tok_copy(k).start()
+    lax.fori_loop(1, slots, start_weights, 0)
+    acc[...] = jnp.zeros_like(acc)
+    own.wait()
+    for k in (1, 3, 2):
+        tok_in(k).wait_recv()
+
+    def c_copy(i):
+        return send(cs.at[i], cr.at[i], c_send.at[i], c_recv.at[i], core_peer)
+
+    def x_copy(i):
+        return send(xs.at[i], xr.at[i], x_send.at[i], x_recv.at[i], x_peer)
+
+    def hx_copy(i):
+        return send(hid.at[i, pl.ds(0, q)], hid.at[i, pl.ds(q, q)], hx_send.at[i], hx_recv.at[i], x_peer)
+
+    def h0_copy(i):
+        return send(hid.at[i, pl.ds(0, h)], hid.at[i, pl.ds(h, h)], h0_send.at[i], h0_recv.at[i], core_peer)
+
+    def project(i):
+        gate_copy(i).wait()
+        up_copy(i).wait()
+        t = tok[...].reshape(T, tok.shape[2])
+        for side, w in enumerate((gate_v, up_v)):
+            p = jnp.dot(t, w[i % slots], preferred_element_type=jnp.float32)
+            at = slice(side * WIDTH, (side + 1) * WIDTH)
+            pown[i, :, at] = p[:h]
+            cs[i, :, at] = p[h:].astype(jnp.bfloat16)
+        c_copy(i).start()
+
+        @pl.when(i + slots < chunks)
+        def _():
+            start_weights(i + slots, 0)
+
+        @pl.when(i == max(chunks - slots - 1, 0))
+        def _():
+            lax.fori_loop(0, chunks, start_down, 0)
+
+    def add_core(i):
+        c_copy(i).wait_recv()
+        s = pown[i] + cr[i].astype(jnp.float32)
+        sown[i] = s[:q]
+        xs[i] = s[q:].astype(jnp.bfloat16)
+        x_copy(i).start()
+
+    def add_x(i):
+        x_copy(i).wait_recv()
+        s = sown[i] + xr[i].astype(jnp.float32)
+        gate, up = s[:, :WIDTH], s[:, WIDTH:]
+        hid[i, pl.ds(0, q), :] = (gate / (1.0 + jnp.exp(-gate)) * up).astype(jnp.bfloat16)
+        hx_copy(i).start()
+
+    def spread(i):
+        hx_copy(i).wait_recv()
+        h0_copy(i).start()
+
+    def contract(i):
+        down_copy(i).wait()
+        h0_copy(i).wait_recv()
+        acc[...] += jnp.dot(hid[i], down_v[i], preferred_element_type=jnp.float32)
+
+    stages = ((spread, 18), (add_x, 10), (add_core, 2), (project, 0), (contract, 20))
+
+    def step(t, carry):
+        for stage, lag in stages:
+            i = t - lag
+            pl.when(jnp.logical_and(i >= 0, i < chunks))(functools.partial(stage, i))
+        return carry
+
+    lax.fori_loop(0, chunks + 20, step, 0)
+
+    def out_copy(k):
+        row = (r + k) % 4
+        return send(obuf.at[place(row)], zr.at[k - 1], oz_send.at[k - 1], oz_recv.at[k - 1], {"row": row})
+
+    obuf[...] = acc[...].astype(jnp.bfloat16).reshape(obuf.shape)
+    for k in (2, 1, 3):
+        out_copy(k).start()
+
+    def drain(i, carry):
+        for copy in (c_copy, x_copy, hx_copy, h0_copy):
+            copy(i).wait_send()
+        return carry
+
+    lax.fori_loop(0, chunks, drain, 0)
+    for k in (1, 2, 3):
+        tok_copy(k).wait_send()
+    total = acc[pl.ds(pl.multiple_of(place(r) * b, b), b), :]
+    for k in (1, 3, 2):
+        out_copy(k).wait_recv()
+        total = total + zr[k - 1].astype(jnp.float32)
+    out_ref[...] = total.astype(jnp.bfloat16)
+    for k in (1, 2, 3):
+        out_copy(k).wait_send()
+
+
+def fused(tokens, gate_weight, up_weight, down_weight):
+    b, k = tokens.shape
+    units = gate_weight.shape[1]
+    n = down_weight.shape[1]
+    chunks = units // WIDTH
+    slots = min(SLOTS, chunks)
+    T = 4 * b
+    q, h = b, 2 * b
+    bf16, f32 = jnp.bfloat16, jnp.float32
+    dma = pltpu.SemaphoreType.DMA
+    per_chunk = dma((chunks,))
+    return pl.pallas_call(
+        kernel,
+        out_shape=jax.ShapeDtypeStruct((b, n), bf16),
+        in_specs=[pl.BlockSpec(memory_space=pl.ANY)] * 4,
+        out_specs=pl.BlockSpec(memory_space=pltpu.VMEM),
+        scratch_shapes=[
+            pltpu.VMEM((4, b, k), bf16),
+            pltpu.VMEM((slots, k, WIDTH), bf16),
+            pltpu.VMEM((slots, k, WIDTH), bf16),
+            pltpu.VMEM((chunks, WIDTH, n), bf16),
+            pltpu.VMEM((chunks, h, 2 * WIDTH), f32),
+            pltpu.VMEM((chunks, h, 2 * WIDTH), bf16),
+            pltpu.VMEM((chunks, h, 2 * WIDTH), bf16),
+            pltpu.VMEM((chunks, q, 2 * WIDTH), f32),
+            pltpu.VMEM((chunks, q, 2 * WIDTH), bf16),
+            pltpu.VMEM((chunks, q, 2 * WIDTH), bf16),
+            pltpu.VMEM((chunks, T, WIDTH), bf16),
+            pltpu.VMEM((T, n), f32),
+            pltpu.VMEM((4, b, n), bf16),
+            pltpu.VMEM((3, b, n), bf16),
+            dma,
+            dma((slots,)),
+            dma((slots,)),
+            per_chunk,
+            dma((3,)),
+            dma((3,)),
+        ]
+        + [per_chunk] * 8
+        + [dma((3,)), dma((3,))],
+        compiler_params=pltpu.CompilerParams(
+            collective_id=0, has_side_effects=True, vmem_limit_bytes=60 * 2**20
+        ),
+        cost_estimate=pl.CostEstimate(
+            flops=6 * T * k * units, bytes_accessed=6 * k * units, transcendentals=q * units
+        ),
+    )(tokens, gate_weight, up_weight, down_weight)
+
+
+def fits(mesh, tokens, gate_weight, down_weight):
+    s = mesh.shape
+    if (s["groups"], s["row"], s["col"]) != (2, 4, 4):
+        return False
+    b, k = tokens.shape[0] // 8, tokens.shape[1] // 4
+    units, n = gate_weight.shape[1] // 4, down_weight.shape[1] // 4
+    held = 4 * SLOTS * k * WIDTH + 2 * units * n + 26 * b * units + 40 * b * (k + n)
+    return b % 16 == 0 and k % 128 == 0 and units % WIDTH == 0 and n % 128 == 0 and held < 57 * 2**20
+
+
 def solution(mesh):
-    return jax.shard_map(
-        on_device,
+    specs = dict(
         mesh=mesh,
         in_specs=(P(("groups", "row"), "col"), P("col", "row"), P("col", "row"), P("row", "col")),
         out_specs=P(("groups", "row"), "col"),
         check_vma=False,
     )
+
+    def layer(tokens, gate_weight, up_weight, down_weight):
+        body = fused if fits(mesh, tokens, gate_weight, down_weight) else plain
+        return jax.shard_map(body, **specs)(tokens, gate_weight, up_weight, down_weight)
+
+    return layer

time: 134 us -> 51.4 us (0.38)
  waiting for transfers between devices: 66.5 us -> 0 us
  Pallas kernels: 0 us -> 49.8 us
  matrix products: 34.7 us -> 0 us
  blocking collectives: 15.8 us -> 0 us
  between operations: 13.4 us -> 0.01 us
  other arithmetic: 2.97 us -> 0 us
  local copies, waits for them, and re-layouts: 0 us -> 1.47 us
    pallas_call x0 -> x1, Pallas kernels: none -> 49.8 us  [fused(): pl.pallas_call(kernel, out_shape=jax.ShapeDtypeStruct((b, n), bf16), in_s...]
    psum x1 -> x0, waiting for transfers between devices: 46.6 us -> none  [on_device(): summed = lax.psum(partials.astype(jnp.bfloat16), 'col').astype(jnp.float32)]
    dot_general x3 -> x0, matrix products: 34.7 us -> none  [the longest x1 12 us: on_device(): jnp.dot(hidden, down_weight, preferred_element_type=jnp.float32)]
    reduce_scatter x1 -> x0, waiting for transfers between devices: 19.9 us -> none  [on_device(): lax.psum_scatter(jnp.dot(hidden, down_weight, preferred_element_type=jnp....]
    all_gather x1 -> x0, blocking collectives: 15.8 us -> none  [on_device(): portion = lax.all_gather(tokens, 'row', axis=0, tiled=True)]
    convert_element_type x1 -> x0, other arithmetic: 1.67 us -> none  [on_device(): summed = lax.psum(partials.astype(jnp.bfloat16), 'col').astype(jnp.float32)]
    unnamed x0 -> x1, local copies, waits for them, and re-layouts: none -> 1.47 us
  transfers between devices with their start and end apart: 2 -> 0, of which waited for: 2 -> 0; matrix products, arithmetic and copies ran while one was open for 0% -> 0% of each run, Pallas kernels for 0% -> 0%
where the time goes in v2:
time: 51.4 us; the launch traced here: 51.3 us
  Pallas kernels  49.8 us (97%)
  local copies, waits for them, and re-layouts  1.47 us (3%)
    pallas_call x1, Pallas kernels, fused(): pl.pallas_call(kernel, out_shape=jax.ShapeDtypeStruct((b, n), bf16), in_s...  49.8 us
    unnamed x1, local copies, waits for them, and re-layouts  1.47 us

profile of v2, /device:TPU:0, one launch (start us, length us, event | category | flops | bytes accessed | tf_op | source)
XLA Modules:
  0.0 51.3 jit_solution(11871833272776249950)
XLA Ops:
  0.0 49.8 %shard_map.46 = bf16[16,2048]{1,0:T(8,128)(2,1)} custom-call(bf16[16,2048]{1,0:T(8,128)(2,1)} %tok_hbm.1, bf16[2048,6656]{1,0:T(8,128)(2,1)} %gate_hbm.1, bf16[2048,6656]{1,0:T(8,128)(2,1)} %up_hbm.1, bf16[6656,2048]{1,0:T(8,128)(2,1)} %down_hbm.1), custom_call_target="tpu_custom_call" | custom-call | flops 5234491392 | bytes 81788928 | tf_op jit(solution)/shard_map/pallas_call | solution.py:207
  49.8 1.5 %copy.6 = bf16[16,2048]{1,0:T(8,128)(2,1)} copy(bf16[16,2048]{1,0:T(8,128)(2,1)} %shard_map.46) | data formatting | bytes 131072

commit v3 on v2

--- a/solution.py
+++ b/solution.py
@@ -34,7 +34,7 @@
 
 def kernel(
     tok_hbm, gate_hbm, up_hbm, down_hbm, out_ref,
-    tok, gate_v, up_v, down_v, pown, cs, cr, sown, xs, xr, hid, acc, obuf, zr,
+    tok, pair_v, down_v, pown, cs, cr, sown, xs, xr, hid, acc, obuf, zr,
     own_sem, gate_sem, up_sem, down_sem, tz_send, tz_recv,
     c_send, c_recv, x_send, x_recv, hx_send, hx_recv, h0_send, h0_recv, oz_send, oz_recv,
 ):
@@ -43,7 +43,7 @@
     core_peer = {"col": x * 2 + (1 - core)}
     x_peer = {"col": (1 - x) * 2 + core}
     b = tok_hbm.shape[0]
-    slots = gate_v.shape[0]
+    slots = pair_v.shape[0]
     chunks = down_v.shape[0]
     T = 4 * b
     q, h = b, 2 * b
@@ -60,11 +60,11 @@
 
     def gate_copy(i):
         at = pl.ds(pl.multiple_of(i * WIDTH, WIDTH), WIDTH)
-        return pltpu.make_async_copy(gate_hbm.at[:, at], gate_v.at[i % slots], gate_sem.at[i % slots])
+        return pltpu.make_async_copy(gate_hbm.at[:, at], pair_v.at[i % slots, :, pl.ds(0, WIDTH)], gate_sem.at[i % slots])
 
     def up_copy(i):
         at = pl.ds(pl.multiple_of(i * WIDTH, WIDTH), WIDTH)
-        return pltpu.make_async_copy(up_hbm.at[:, at], up_v.at[i % slots], up_sem.at[i % slots])
+        return pltpu.make_async_copy(up_hbm.at[:, at], pair_v.at[i % slots, :, pl.ds(WIDTH, WIDTH)], up_sem.at[i % slots])
 
     def down_copy(i):
         rows = pl.ds(pl.multiple_of(i * WIDTH, WIDTH), WIDTH)
@@ -120,11 +120,9 @@
         gate_copy(i).wait()
         up_copy(i).wait()
         t = tok[...].reshape(T, tok.shape[2])
-        for side, w in enumerate((gate_v, up_v)):
-            p = jnp.dot(t, w[i % slots], preferred_element_type=jnp.float32)
-            at = slice(side * WIDTH, (side + 1) * WIDTH)
-            pown[i, :, at] = p[:h]
-            cs[i, :, at] = p[h:].astype(jnp.bfloat16)
+        p = jnp.dot(t, pair_v[i % slots], preferred_element_type=jnp.float32)
+        pown[i] = p[:h]
+        cs[i] = p[h:].astype(jnp.bfloat16)
         c_copy(i).start()
 
         @pl.when(i + slots < chunks)
@@ -156,9 +154,14 @@
     def contract(i):
         down_copy(i).wait()
         h0_copy(i).wait_recv()
-        acc[...] += jnp.dot(hid[i], down_v[i], preferred_element_type=jnp.float32)
-
-    stages = ((spread, 18), (add_x, 10), (add_core, 2), (project, 0), (contract, 20))
+
+        @pl.when(i % 2 == 1)
+        def _():
+            first = pl.ds(i - 1, 2)
+            two = jnp.concatenate([hid[i - 1], hid[i]], axis=1)
+            acc[...] += jnp.dot(two, down_v[first].reshape(2 * WIDTH, down_v.shape[2]), preferred_element_type=jnp.float32)
+
+    stages = ((spread, 24), (add_x, 14), (add_core, 4), (project, 0), (contract, 26))
 
     def step(t, carry):
         for stage, lag in stages:
@@ -166,7 +169,7 @@
             pl.when(jnp.logical_and(i >= 0, i < chunks))(functools.partial(stage, i))
         return carry
 
-    lax.fori_loop(0, chunks + 20, step, 0)
+    lax.fori_loop(0, chunks + 26, step, 0)
 
     def out_copy(k):
         row = (r + k) % 4
@@ -211,8 +214,7 @@
         out_specs=pl.BlockSpec(memory_space=pltpu.VMEM),
         scratch_shapes=[
             pltpu.VMEM((4, b, k), bf16),
-            pltpu.VMEM((slots, k, WIDTH), bf16),
-            pltpu.VMEM((slots, k, WIDTH), bf16),
+            pltpu.VMEM((slots, k, 2 * WIDTH), bf16),
             pltpu.VMEM((chunks, WIDTH, n), bf16),
             pltpu.VMEM((chunks, h, 2 * WIDTH), f32),
             pltpu.VMEM((chunks, h, 2 * WIDTH), bf16),
@@ -249,7 +251,7 @@
     b, k = tokens.shape[0] // 8, tokens.shape[1] // 4
     units, n = gate_weight.shape[1] // 4, down_weight.shape[1] // 4
     held = 4 * SLOTS * k * WIDTH + 2 * units * n + 26 * b * units + 40 * b * (k + n)
-    return b % 16 == 0 and k % 128 == 0 and units % WIDTH == 0 and n % 128 == 0 and held < 57 * 2**20
+    return b % 16 == 0 and k % 128 == 0 and units % (2 * WIDTH) == 0 and n % 128 == 0 and held < 57 * 2**20
 
 
 def solution(mesh):

time: 51.4 us -> 47.9 us (0.932)
  Pallas kernels: 49.8 us -> 46.2 us
    pallas_call x1, Pallas kernels: 49.8 us -> 46.2 us  [fused(): pl.pallas_call(kernel, out_shape=jax.ShapeDtypeStruct((b, n), bf16), in_s...]
where the time goes in v3:
time: 47.9 us; the launch traced here: 47.7 us
  Pallas kernels  46.2 us (96%)
  local copies, waits for them, and re-layouts  1.47 us (3%)
    pallas_call x1, Pallas kernels, fused(): pl.pallas_call(kernel, out_shape=jax.ShapeDtypeStruct((b, n), bf16), in_s...  46.2 us
    unnamed x1, local copies, waits for them, and re-layouts  1.47 us

profile of v3, /device:TPU:0, one launch (start us, length us, event | category | flops | bytes accessed | tf_op | source)
XLA Modules:
  0.0 47.7 jit_solution(8364401470610052638)
XLA Ops:
  0.0 46.2 %shard_map.46 = bf16[16,2048]{1,0:T(8,128)(2,1)} custom-call(bf16[16,2048]{1,0:T(8,128)(2,1)} %tok_hbm.1, bf16[2048,6656]{1,0:T(8,128)(2,1)} %gate_hbm.1, bf16[2048,6656]{1,0:T(8,128)(2,1)} %up_hbm.1, bf16[6656,2048]{1,0:T(8,128)(2,1)} %down_hbm.1), custom_call_target="tpu_custom_call" | custom-call | flops 5234491392 | bytes 81788928 | tf_op jit(solution)/shard_map/pallas_call | solution.py:210
  46.3 1.5 %copy.6 = bf16[16,2048]{1,0:T(8,128)(2,1)} copy(bf16[16,2048]{1,0:T(8,128)(2,1)} %shard_map.46) | data formatting | bytes 131072
